TPU v7x, 128 devices: a whole 4x4x4 slice. The times are simulated.
128 devices in a mesh: section: 2 (over core), ctx: 16 (over y, x), tp: 4 (over z).
Axes of the slice: x: 4, y: 4, z: 4, core: 2. Of those that a mesh axis runs over, the one named last changes fastest.
Arguments:
- inputs: bfloat16 [2, 4096, 768], P(None, 'ctx'), may hold values from -6 to 6
- cotangent: bfloat16 [2, 4096, 768], P(None, 'ctx'), may hold values from -6 to 6
- segments: int32 [2, 4096], P(None, 'ctx'), may hold values from 0 to 5, never falling along the last dimension, each value on 1 to 2048 neighbouring positions
- w_qkv: bfloat16 [2, 768, 2304], P('section', 'ctx', 'tp'), may hold values from -0.21875 to 0.21875
- b_qkv: bfloat16 [2, 2304], P('section', 'tp'), may hold values from -3 to 3
- w_out: bfloat16 [2, 768, 768], P('section', 'ctx', 'tp'), may hold values from -1.25 to 1.25
- w_up: bfloat16 [2, 768, 3072], P('section', 'ctx', 'tp'), may hold values from -0.21875 to 0.21875
- b_up: bfloat16 [2, 3072], P('section', 'tp'), may hold values from -3 to 3
- w_down: bfloat16 [2, 768, 3072], P('section', 'ctx', 'tp'), may hold values from -0.109375 to 0.109375
- b_out: bfloat16 [2, 768], P('section'), may hold values from -3 to 3
- norm_gain: bfloat16 [2, 2, 768], P('section'), may hold values from 0.5 to 1.5
- norm_bias: bfloat16 [2, 2, 768], P('section'), may hold values from -2 to 2
Outputs:
- hidden_out: bfloat16 [2, 2, 4096, 768], P('section', None, 'ctx')
- input_grad: float32 [2, 2, 4096, 768], P('section', None, 'ctx')
- grad_w_qkv: float32 [2, 768, 2304], P('section', 'ctx', 'tp')
- grad_b_qkv: float32 [2, 2304], P('section', 'tp')
- grad_w_out: float32 [2, 768, 768], P('section', 'ctx', 'tp')
- grad_w_up: float32 [2, 768, 3072], P('section', 'ctx', 'tp')
- grad_b_up: float32 [2, 3072], P('section', 'tp')
- grad_w_down: float32 [2, 768, 3072], P('section', 'ctx', 'tp')
- grad_b_out: float32 [2, 768], P('section')
- grad_norm_gain: float32 [2, 2, 768], P('section')
- grad_norm_bias: float32 [2, 2, 768], P('section')
Inputs may be any that keep to these rules, and one draw needn't show every extreme that they name: `segments`: document ids of each micro-batch never fall along its tokens; every id occurs, each document has 1 to 2048 tokens and one has exactly 2048.
All inputs are finite; a program needn't handle non-finite values.
Results may differ from a plain program's by a relative error of at most 0.02.
Values may be sent and summed in bfloat16 or wider, within the bound.
No kernel may reach another device: no remote copies, remote signals or barrier semaphores. Data moves between devices by JAX's collectives and lax.ppermute only.
A program may use at most 128 MiB of HBM per device.

v0:
```python
import math

import jax
import jax.numpy as jnp
from jax import lax
from jax.sharding import PartitionSpec as P

HEAD_DIM = 64
ROT = 16


def passed_along(value, axis, steps):
    count = lax.axis_size(axis)
    leading, last = (max(0, -steps), min(count, count - steps))
    return lax.ppermute(value, axis, [(source, source + steps) for source in range(leading, last)])


def layer_norm(values, gain_vec, shift_vec):
    center = values - jnp.mean(values, axis=-1, keepdims=True)
    spread = jnp.mean(center * center, axis=-1, keepdims=True)
    inverse = lax.rsqrt(spread + 1e-05)
    normed = center * inverse
    return (normed * gain_vec + shift_vec, normed, inverse)


def norm_backward(grad_norm, normed, inverse, gain_vec):
    scaled = grad_norm * gain_vec
    return inverse * (
        scaled
        - jnp.mean(scaled, axis=-1, keepdims=True)
        - normed * jnp.mean(scaled * normed, axis=-1, keepdims=True)
    )


def angle_table(places):
    frequency = jnp.exp(-(jnp.arange(ROT // 2, dtype=jnp.float32) * (2.0 / ROT)) * jnp.log(10000.0))
    return places[:, None] * frequency[None, :]


def rotate(values, angles, sign_factor):
    half_rot = angles.shape[-1]
    cosine = jnp.cos(angles)
    sine_vals = sign_factor * jnp.sin(angles)
    cosine = jnp.concatenate([cosine, cosine], -1)[:, None, :]
    sine_vals = jnp.concatenate([sine_vals, sine_vals], -1)[:, None, :]
    rot_part = values[..., : 2 * half_rot]
    turned = jnp.concatenate([-rot_part[..., half_rot:], rot_part[..., :half_rot]], -1)
    return jnp.concatenate(
        [rot_part * cosine + turned * sine_vals, values[..., 2 * half_rot :]], -1
    )


def gelu_exact(values):
    return 0.5 * values * (1.0 + jax.scipy.special.erf(values * 0.7071067811865476))


def gelu_slope(values):
    return (
        0.5 * (1.0 + jax.scipy.special.erf(values * 0.7071067811865476))
        + values * jnp.exp(-0.5 * values * values) * 0.3989422804014327
    )


def dot_last(left, right):
    return lax.dot_general(
        left, right, (((1,), (1,)), ((), ())), preferred_element_type=jnp.float32
    )


def dot_first(left, right):
    return lax.dot_general(
        left, right, (((0,), (0,)), ((), ())), preferred_element_type=jnp.float32
    )


def stack_items(*items):
    return jnp.stack(items)


def per_device(
    inputs,
    cotangent,
    segments,
    w_qkv,
    b_qkv,
    w_out,
    w_up,
    b_up,
    w_down,
    b_out,
    norm_gain,
    norm_bias,
):
    section_rank = lax.axis_index("section")
    place_rank = lax.axis_index("ctx")
    micro_count = inputs.shape[0]
    tok_rows = inputs.shape[1]
    model_width = inputs.shape[2]
    qkv_cols = w_qkv.shape[2]
    up_cols = w_up.shape[2]
    att_cols = w_out.shape[2]
    head_count = qkv_cols // (3 * HEAD_DIM)
    head_cols = head_count * HEAD_DIM
    seq_length = tok_rows * lax.axis_size("ctx")
    score_scale = HEAD_DIM ** (-0.5)
    positions = place_rank * tok_rows + jnp.arange(tok_rows, dtype=jnp.int32)
    first_place = place_rank * tok_rows
    last_place = first_place + tok_rows - 1
    angles = angle_table(positions.astype(jnp.float32))
    weight_in = jnp.concatenate([w_qkv[0], w_up[0]], 1)
    weight_out = jnp.concatenate([w_out[0], w_down[0]], 1)
    bias_qkv = b_qkv[0].astype(jnp.float32)
    bias_up = b_up[0].astype(jnp.float32)
    bias_out = b_out[0].astype(jnp.float32)
    gains = norm_gain[0].astype(jnp.float32)
    shifts = norm_bias[0].astype(jnp.float32)
    forward_outs = []
    kept_all = []
    received = jnp.zeros((tok_rows, model_width), jnp.bfloat16)
    for tick_index in range(micro_count + 1):
        own_slice = inputs[min(tick_index, micro_count - 1)]
        layer_in = jnp.where(section_rank == 0, own_slice, received)
        seg_ids = segments[jnp.clip(tick_index - section_rank, 0, micro_count - 1)]
        forward_values = layer_in.astype(jnp.float32)
        forward_first_norm, _, _ = layer_norm(forward_values, gains[0], shifts[0])
        forward_second_norm, _, _ = layer_norm(forward_values, gains[1], shifts[1])
        forward_first_in = forward_first_norm.astype(jnp.bfloat16)
        forward_second_in = forward_second_norm.astype(jnp.bfloat16)
        weight_piece = lax.all_gather(weight_in, "ctx", axis=0, tiled=True)
        piece_rows = weight_piece.shape[0]
        packed = jnp.dot(
            forward_first_in, weight_piece[:, :qkv_cols], preferred_element_type=jnp.float32
        )
        forward_hidden_pre = jnp.dot(
            forward_second_in, weight_piece[:, qkv_cols:], preferred_element_type=jnp.float32
        )
        packed = (packed + bias_qkv).reshape(tok_rows, head_count, 3, HEAD_DIM)
        forward_hidden_pre = forward_hidden_pre + bias_up
        forward_query_low = rotate(packed[:, :, 0], angles, 1.0).astype(jnp.bfloat16)
        key_low = rotate(packed[:, :, 1], angles, 1.0).astype(jnp.bfloat16)
        value_low = packed[:, :, 2].astype(jnp.bfloat16)
        forward_keyval = jnp.concatenate(
            [key_low.reshape(tok_rows, head_cols), value_low.reshape(tok_rows, head_cols)], 1
        )
        attend_query_low = forward_query_low
        start_state = (
            jnp.full((head_count, tok_rows), -1e30, jnp.float32),
            jnp.zeros((head_count, tok_rows), jnp.float32),
            jnp.zeros((tok_rows, head_count, HEAD_DIM), jnp.float32),
        )

        def add_keys(carry_state, pieces, start_row):
            kv_piece, seg_piece = pieces
            piece_rows = kv_piece.shape[0]

            def add_active(carry_state):
                key_heads = kv_piece[:, :head_cols].reshape(piece_rows, head_count, HEAD_DIM)
                value_heads = kv_piece[:, head_cols:].reshape(piece_rows, head_count, HEAD_DIM)
                scores = (
                    jnp.einsum(
                        "qhd,khd->hqk",
                        attend_query_low,
                        key_heads,
                        preferred_element_type=jnp.float32,
                    )
                    * score_scale
                )
                key_places = jnp.arange(piece_rows, dtype=jnp.int32)
                allowed = (key_places[None, :] <= positions[:, None]) & (
                    seg_piece[None, :] == seg_ids[:, None]
                )
                scores = jnp.where(allowed[None], scores, -1e30)
                row_top, row_total, weighted = carry_state
                new_top = jnp.maximum(row_top, jnp.max(scores, axis=-1))
                weights = jnp.where(allowed[None], jnp.exp(scores - new_top[..., None]), 0.0)
                factor = jnp.exp(row_top - new_top)
                row_total = jnp.sum(weights, axis=-1)
                weighted = weighted * factor.T[:, :, None] + jnp.einsum(
                    "hqk,khd->qhd",
                    weights.astype(jnp.bfloat16),
                    value_heads,
                    preferred_element_type=jnp.float32,
                )
                return (new_top, row_total, weighted)

            def add_skipped(carry_state):
                return carry_state

            return lax.cond(start_row <= last_place, add_active, add_skipped, carry_state)

        row_top, row_total, weighted = add_keys(
            start_state,
            (
                lax.all_gather(forward_keyval, "ctx", axis=0, tiled=True),
                lax.all_gather(seg_ids, "ctx", axis=0, tiled=True),
            ),
            jnp.int32(0),
        )
        forward_mixed_heads = weighted / row_total.T[:, :, None]
        forward_logsum = row_top + jnp.log(row_total)
        forward_mixed_low = forward_mixed_heads.reshape(tok_rows, head_cols).astype(jnp.bfloat16)
        forward_hidden = gelu_exact(forward_hidden_pre).astype(jnp.bfloat16)

        def add_out(weight_piece):
            return dot_last(forward_mixed_low, weight_piece[:, :att_cols]) + dot_last(
                forward_hidden, weight_piece[:, att_cols:]
            )

        branches = add_out(lax.all_gather(weight_out, "ctx", axis=0, tiled=True))
        branch_total = lax.psum(branches.astype(jnp.bfloat16), "tp").astype(jnp.float32)
        result = (forward_values + branch_total + bias_out).astype(jnp.bfloat16)
        result, kept_items = (
            result,
            (
                layer_in,
                forward_query_low,
                forward_keyval,
                forward_mixed_heads,
                forward_logsum,
                forward_hidden_pre,
            ),
        )
        forward_outs.append(result)
        kept_all.append(kept_items)
        if tick_index < micro_count:
            received = passed_along(result, "section", 1)
    kept_stack = jax.tree.map(stack_items, *kept_all)
    in_total = jnp.zeros((model_width, qkv_cols + up_cols), jnp.float32)
    out_total = jnp.zeros((model_width, att_cols + up_cols), jnp.float32)
    small_total = None
    input_grads = []
    returned = jnp.zeros((tok_rows, model_width), jnp.bfloat16)
    for tick_index in range(micro_count + 1):
        micro_index = tick_index - 1 + section_rank
        is_valid = (micro_index >= 0) & (micro_index < micro_count)
        safe_index = jnp.clip(micro_index, 0, micro_count - 1)
        own_slice = cotangent[min(tick_index, micro_count - 1)]
        incoming = jnp.where(section_rank == 1, own_slice, returned).astype(jnp.float32)
        grad_top = jnp.where(is_valid, incoming, 0.0)
        kept_items = tuple((item[safe_index + section_rank] for item in kept_stack))
        backward_seg_ids = segments[safe_index]
        backward_layer_in, query_low, keyval, mixed_heads, logsum, hidden_pre = kept_items
        values = backward_layer_in.astype(jnp.float32)
        first_norm, normed_first, inverse_first = layer_norm(values, gains[0], shifts[0])
        second_norm, normed_second, inverse_second = layer_norm(values, gains[1], shifts[1])
        first_in = first_norm.astype(jnp.bfloat16)
        second_in = second_norm.astype(jnp.bfloat16)
        grad_low = grad_top.astype(jnp.bfloat16)
        mixed_low = mixed_heads.reshape(tok_rows, head_cols).astype(jnp.bfloat16)
        hidden = gelu_exact(hidden_pre).astype(jnp.bfloat16)
        add_weight_piece = lax.all_gather(weight_out, "ctx", axis=0, tiled=True)
        grad_mixed = jnp.dot(
            grad_low, add_weight_piece[:, :att_cols], preferred_element_type=jnp.float32
        )
        grad_hidden = jnp.dot(
            grad_low, add_weight_piece[:, att_cols:], preferred_element_type=jnp.float32
        )
        grad_pre = (grad_hidden * gelu_slope(hidden_pre)).astype(jnp.bfloat16)
        grad_heads = grad_mixed.astype(jnp.bfloat16).reshape(tok_rows, head_count, HEAD_DIM)
        row_delta = jnp.sum(grad_heads.astype(jnp.float32) * mixed_heads, axis=-1).T
        whole_kv = lax.all_gather(keyval, "ctx", axis=0, tiled=True)
        whole_seg = lax.all_gather(backward_seg_ids, "ctx", axis=0, tiled=True)
        block_rows = math.gcd(seq_length, 512)
        block_count = seq_length // block_rows
        kv_blocks = whole_kv.reshape(block_count, block_rows, 2 * head_cols)
        seg_blocks = whole_seg.reshape(block_count, block_rows)
        starts = jnp.arange(block_count, dtype=jnp.int32) * block_rows

        def block_terms(kv_piece, seg_piece, start_row):
            key_heads = kv_piece[:, :head_cols].reshape(block_rows, head_count, HEAD_DIM)
            value_heads = kv_piece[:, head_cols:].reshape(block_rows, head_count, HEAD_DIM)
            scores = (
                jnp.einsum("qhd,khd->hqk", query_low, key_heads, preferred_element_type=jnp.float32)
                * score_scale
            )
            key_places = start_row + jnp.arange(block_rows, dtype=jnp.int32)
            allowed = (key_places[None, :] <= positions[:, None]) & (
                seg_piece[None, :] == backward_seg_ids[:, None]
            )
            probs = jnp.where(allowed[None], jnp.exp(scores - logsum[..., None]), 0.0)
            grad_probs = jnp.einsum(
                "qhd,khd->hqk", grad_heads, value_heads, preferred_element_type=jnp.float32
            )
            grad_scores = (probs * (grad_probs - row_delta[..., None])).astype(jnp.bfloat16)
            return (key_heads, probs, grad_scores)

        def key_block(grad_query, items):
            kv_piece, seg_piece, start_row = items

            def key_active(grad_query):
                key_heads, probs, grad_scores = block_terms(kv_piece, seg_piece, start_row)
                grad_value = jnp.einsum(
                    "hqk,qhd->khd",
                    probs.astype(jnp.bfloat16),
                    grad_heads,
                    preferred_element_type=jnp.float32,
                )
                grad_query = (
                    grad_query
                    + jnp.einsum(
                        "hqk,khd->qhd", grad_scores, key_heads, preferred_element_type=jnp.float32
                    )
                    * score_scale
                )
                grad_key = (
                    jnp.einsum(
                        "hqk,qhd->khd", grad_scores, query_low, preferred_element_type=jnp.float32
                    )
                    * score_scale
                )
                return (
                    grad_query,
                    jnp.concatenate(
                        [
                            grad_key.reshape(block_rows, head_cols),
                            grad_value.reshape(block_rows, head_cols),
                        ],
                        1,
                    ),
                )

            def key_skipped(grad_query):
                return (grad_query, jnp.zeros((block_rows, 2 * head_cols), jnp.float32))

            return lax.cond(start_row <= last_place, key_active, key_skipped, grad_query)

        grad_query, grad_kv = lax.scan(
            key_block,
            jnp.zeros((tok_rows, head_count, HEAD_DIM), jnp.float32),
            (kv_blocks, seg_blocks, starts),
        )
        grad_kv = lax.psum_scatter(
            grad_kv.reshape(seq_length, 2 * head_cols).astype(jnp.bfloat16),
            "ctx",
            scatter_dimension=0,
            tiled=True,
        ).astype(jnp.float32)
        grad_key = rotate(
            grad_kv[:, :head_cols].reshape(tok_rows, head_count, HEAD_DIM), angles, -1.0
        )
        grad_value = grad_kv[:, head_cols:].reshape(tok_rows, head_count, HEAD_DIM)
        grad_query = rotate(grad_query, angles, -1.0)
        grad_packed = (
            jnp.stack([grad_query, grad_key, grad_value], 2)
            .reshape(tok_rows, qkv_cols)
            .astype(jnp.bfloat16)
        )
        in_grad = jnp.concatenate(
            [dot_first(first_in, grad_packed), dot_first(second_in, grad_pre)], 1
        )
        out_grad = jnp.concatenate([dot_first(grad_low, mixed_low), dot_first(grad_low, hidden)], 1)
        back_weight_piece = lax.all_gather(weight_in, "ctx", axis=0, tiled=True)
        norm_terms = jnp.stack(
            [
                dot_last(grad_packed, back_weight_piece[:, :qkv_cols]),
                dot_last(grad_pre, back_weight_piece[:, qkv_cols:]),
            ]
        )
        norm_terms = lax.psum(norm_terms.astype(jnp.bfloat16), "tp").astype(jnp.float32)
        grad_input = (
            grad_top
            + norm_backward(norm_terms[0], normed_first, inverse_first, gains[0])
            + norm_backward(norm_terms[1], normed_second, inverse_second, gains[1])
        )
        backward_gain_grad = jnp.stack(
            [
                jnp.sum(norm_terms[0] * normed_first, axis=0),
                jnp.sum(norm_terms[1] * normed_second, axis=0),
            ]
        )
        backward_shift_grad = jnp.stack(
            [jnp.sum(norm_terms[0], axis=0), jnp.sum(norm_terms[1], axis=0)]
        )
        small_terms = (
            jnp.sum(grad_packed.astype(jnp.float32), axis=0),
            jnp.sum(grad_pre.astype(jnp.float32), axis=0),
            jnp.sum(grad_top, axis=0),
            backward_gain_grad,
            backward_shift_grad,
        )
        grad_input, in_grad, out_grad, small_terms = (grad_input, in_grad, out_grad, small_terms)
        in_total = in_total + in_grad
        out_total = out_total + out_grad
        if small_total is None:
            small_total = small_terms
        else:
            small_total = tuple(
                (left_item + right_item for left_item, right_item in zip(small_total, small_terms))
            )
        input_grads.append(grad_input)
        if tick_index < micro_count:
            returned = passed_along(grad_input.astype(jnp.bfloat16), "section", -1)
    summed_in, summed_out = (
        lax.psum_scatter(
            in_total.astype(jnp.bfloat16), "ctx", scatter_dimension=0, tiled=True
        ).astype(jnp.float32),
        lax.psum_scatter(
            out_total.astype(jnp.bfloat16), "ctx", scatter_dimension=0, tiled=True
        ).astype(jnp.float32),
    )
    bias_qkv_grad, bias_up_grad, bias_out_grad, gain_grad, shift_grad = lax.psum(small_total, "ctx")
    hidden_out = lax.dynamic_slice_in_dim(jnp.stack(forward_outs), section_rank, micro_count, 0)[
        None
    ]
    input_grad = lax.dynamic_slice_in_dim(jnp.stack(input_grads), 1 - section_rank, micro_count, 0)[
        None
    ]
    return (
        hidden_out,
        input_grad,
        summed_in[:, :qkv_cols][None],
        bias_qkv_grad[None],
        summed_out[:, :att_cols][None],
        summed_in[:, qkv_cols:][None],
        bias_up_grad[None],
        summed_out[:, att_cols:][None],
        bias_out_grad[None],
        gain_grad[None],
        shift_grad[None],
    )


def solution(mesh):
    placed = (
        P(None, "ctx", None),
        P(None, "ctx", None),
        P(None, "ctx"),
        P("section", "ctx", "tp"),
        P("section", "tp"),
        P("section", "ctx", "tp"),
        P("section", "ctx", "tp"),
        P("section", "tp"),
        P("section", "ctx", "tp"),
        P("section", None),
        P("section", None, None),
        P("section", None, None),
    )
    return jax.shard_map(
        per_device,
        mesh=mesh,
        in_specs=placed,
        out_specs=(
            P("section", None, "ctx", None),
            P("section", None, "ctx", None),
            P("section", "ctx", "tp"),
            P("section", "tp"),
            P("section", "ctx", "tp"),
            P("section", "ctx", "tp"),
            P("section", "tp"),
            P("section", "ctx", "tp"),
            P("section", None),
            P("section", None, None),
            P("section", None, None),
        ),
        check_vma=False,
    )
```

profile of v0, /device:TPU:7, one launch (start us, length us, event | category | flops | bytes accessed | tf_op | source)
XLA Modules:
  0.0 1389.6 jit_solution(14816688322092675793)
XLA Ops:
  13.3 43.5 %all-gather.18.cloned.1.call-done = bf16[768,1344]{1,0:T(8,128)(2,1)} async-done(((bf16[48,1344]{1,0:T(8,128)(2,1)}), bf16[768,1344]{1,0:T(8,128)(2,1)}) %all-gather.18.cloned.1.call-update) | async-done | bytes 2064400 | tf_op jit(solution)/shard_map/all_gather | solution.py:129
  80.1 31.8 %all-gather.20.cloned.1.call-done = bf16[4096,384]{0,1:T(8,128)(2,1)} async-done(((bf16[256,384]{0,1:T(8,128)(2,1)}), bf16[4096,384]{0,1:T(8,128)(2,1)}) %all-gather.20.cloned.1.call-update) | async-done | bytes 3145744 | tf_op jit(solution)/shard_map/all_gather | solution.py:194
  111.9 25.8 %conditional.6 = (f32[3,256]{1,0:T(4,128)}, f32[3,256]{1,0:T(4,128)}, f32[256,3,64]{0,2,1:T(8,128)S(1)}, f32[3,256]{1,0:T(4,128)S(1)}) conditional(s32[]{:T(128)} %convert_element_type.468, () %tuple.92, (s32[256]{0:T(256)}, s32[4096]{0:T(1024)S(1)}, s32[1,256]{1,0:T(1,128)S(1)}, bf16[4096,384]{0,1:T(8,128)(2,1)}, ...), branch_computations={%region_2.3_spmd, %region_3.0_spmd} | conditional | flops 849396480 | bytes 51724320 | solution.py:189
  162.2 41.0 %all-reduce.10.cloned.1.call-done = bf16[256,768]{1,0:T(8,128)(2,1)} async-done(((bf16[256,768]{1,0:T(8,128)(2,1)}), bf16[256,768]{1,0:T(8,128)(2,1)}) %all-reduce.10.cloned.1.call-update) | async-done | bytes 393232 | tf_op jit(solution)/shard_map/psum | solution.py:210
  213.1 19.6 %all-gather.1 = s32[1,4096]{1,0:T(1,128)} all-gather(s32[1,256]{1,0:T(1,128)S(1)} %copy-done.139), channel_id=3, replica_groups=mesh['section'=2,'ctx'=16,'tp'=4] {'ctx'}, dimensions={1}, use_global_device_ids=true | all-gather | bytes 17408 | tf_op jit(solution)/shard_map/all_gather | solution.py:195
  235.8 28.6 %all-gather.24.cloned.1.call-done = bf16[4096,384]{0,1:T(8,128)(2,1)} async-done(((bf16[256,384]{0,1:T(8,128)(2,1)}), bf16[4096,384]{0,1:T(8,128)(2,1)}) %all-gather.24.cloned.1.call-update) | async-done | bytes 3145744 | tf_op jit(solution)/shard_map/all_gather | solution.py:194
  264.3 25.9 %conditional.7 = (f32[3,256]{1,0:T(4,128)}, f32[3,256]{1,0:T(4,128)}, f32[256,3,64]{0,2,1:T(8,128)S(1)}, f32[3,256]{1,0:T(4,128)S(1)}) conditional(s32[]{:T(128)} %convert_element_type.468, () %tuple.94, (s32[256]{0:T(256)}, s32[4096]{0:T(1024)S(1)}, s32[1,256]{1,0:T(1,128)}, bf16[4096,384]{0,1:T(8,128)(2,1)}, ...), branch_computations={%region_9.10_spmd, %region_10.13_spmd} | conditional | flops 849396480 | bytes 51724320 | solution.py:189
  294.6 41.1 %all-reduce.12.cloned.1.call-done = bf16[256,768]{1,0:T(8,128)(2,1)} async-done(((bf16[256,768]{1,0:T(8,128)(2,1)}), bf16[256,768]{1,0:T(8,128)(2,1)}) %all-reduce.12.cloned.1.call-update) | async-done | bytes 393232 | tf_op jit(solution)/shard_map/psum | solution.py:210
  404.4 47.6 %all-gather.26.cloned.1.call-done = bf16[4096,384]{0,1:T(8,128)(2,1)} async-done(((bf16[256,384]{0,1:T(8,128)(2,1)}), bf16[4096,384]{0,1:T(8,128)(2,1)}) %all-gather.26.cloned.1.call-update) | async-done | bytes 3145744 | tf_op jit(solution)/shard_map/all_gather | solution.py:194
  452.0 26.0 %conditional.8 = (f32[3,256]{1,0:T(4,128)}, f32[3,256]{1,0:T(4,128)}, f32[256,3,64]{0,2,1:T(8,128)S(1)}, f32[3,256]{1,0:T(4,128)S(1)}) conditional(s32[]{:T(128)} %convert_element_type.468, () %tuple.96, (s32[256]{0:T(256)}, s32[4096]{0:T(1024)}, s32[1,256]{1,0:T(1,128)}, bf16[4096,384]{0,1:T(8,128)(2,1)}, bf16[256,3,64]{0,2,1:T(8,128)(2,1)}) %tuple.319), branch_computations={%region_16.17_spmd, %region_17.20_spmd} | conditional | flops 849396480 | bytes 52117564 | solution.py:189
  483.4 32.8 %while.48 = (s32[]{:T(128)}, f32[256,3,64]{0,2,1:T(8,128)S(1)}, bf16[8,512,384]{2,1,0:T(8,128)(2,1)}, s32[8]{0:T(128)}, s32[]{:T(128)}, /*index=5*/s32[8,512]{1,...) while((s32[]{:T(128)}, f32[256,3,64]{0,2,1:T(8,128)S(1)}, ...), condition=%wide.region_27.28_spmd.clone, body=%wide.region_24.0_spmd.clone.sunk | while | flops 255886080 | bytes 13063975 | solution.py:327
  524.8 93.0 %reduce-scatter.8.cloned.1.call-done = bf16[256,384]{1,0:T(8,128)(2,1)} async-done(((bf16[4096,384]{1,0:T(8,128)(2,1)}), bf16[256,384]{1,0:T(8,128)(2,1)}) %reduce-scatter.8.cloned.1.call-update) | async-done | bytes 196624 | tf_op jit(solution)/shard_map/reduce_scatter | solution.py:332
  626.7 42.0 %all-reduce.14.cloned.1.call-done = bf16[2,256,768]{2,1,0:T(8,128)(2,1)} async-done(((bf16[2,256,768]{2,1,0:T(8,128)(2,1)}), bf16[2,256,768]{2,1,0:T(8,128)(2,1)}) %all-reduce.14.cloned.1.call-update) | async-done | bytes 786448 | tf_op jit(solution)/shard_map/psum | solution.py:359
  678.5 19.1 %all-gather.5 = s32[1,4096]{1,0:T(1,128)} all-gather(s32[1,256]{1,0:T(1,128)} %get-tuple-element.1477), channel_id=7, replica_groups=mesh['section'=2,'ctx'=16,'tp'=4] {'ctx'}, dimensions={1}, use_global_device_ids=true | all-gather | bytes 17408 | tf_op jit(solution)/shard_map/all_gather | solution.py:262
  700.9 23.6 %all-gather.30.cloned.1.call-done = bf16[1,4096,384]{1,2,0:T(8,128)(2,1)} async-done(((bf16[1,256,384]{1,2,0:T(8,128)(2,1)}), bf16[1,4096,384]{1,2,0:T(8,128)(2,1)}) %all-gather.30.cloned.1.call-update) | async-done | bytes 3145744 | tf_op jit(solution)/shard_map/all_gather | solution.py:261
  741.6 44.9 %while.49 = (s32[]{:T(128)}, f32[256,3,64]{0,2,1:T(8,128)}, bf16[8,512,384]{2,1,0:T(8,128)(2,1)}, s32[8]{0:T(128)}, s32[]{:T(128)}, /*index=5*/s32[8,512]{1,0:T(...) while((s32[]{:T(128)}, f32[256,3,64]{0,2,1:T(8,128)}, ...), condition=%wide.region_40.41_spmd.clone, body=%wide.region_37.40_spmd.clone.sunk | while | flops 255886080 | bytes 13063975 | solution.py:327
  794.0 129.9 %reduce-scatter.10.cloned.1.call-done = bf16[256,384]{1,0:T(8,128)(2,1)} async-done(((bf16[4096,384]{1,0:T(8,128)(2,1)}), bf16[256,384]{1,0:T(8,128)(2,1)}) %reduce-scatter.10.cloned.1.call-update) | async-done | bytes 196624 | tf_op jit(solution)/shard_map/reduce_scatter | solution.py:332
  941.3 38.3 %all-reduce.16.cloned.1.call-done = bf16[2,256,768]{2,1,0:T(8,128)(2,1)} async-done(((bf16[2,256,768]{2,1,0:T(8,128)(2,1)}), bf16[2,256,768]{2,1,0:T(8,128)(2,1)}) %all-reduce.16.cloned.1.call-update) | async-done | bytes 786448 | tf_op jit(solution)/shard_map/psum | solution.py:359
  1015.8 19.4 %all-gather.32.cloned.1.call-done = bf16[1,4096,384]{1,2,0:T(8,128)(2,1)} async-done(((bf16[1,256,384]{1,2,0:T(8,128)(2,1)}), bf16[1,4096,384]{1,2,0:T(8,128)(2,1)}) %all-gather.32.cloned.1.call-update) | async-done | bytes 3145744 | tf_op jit(solution)/shard_map/all_gather | solution.py:261
  1050.8 43.7 %while.50 = (s32[]{:T(128)}, f32[256,3,64]{0,2,1:T(8,128)}, bf16[8,512,384]{2,1,0:T(8,128)(2,1)}, s32[8]{0:T(128)}, s32[]{:T(128)}, /*index=5*/s32[8,512]{1,0:T(...) while((s32[]{:T(128)}, f32[256,3,64]{0,2,1:T(8,128)}, ...), condition=%wide.region_53.54_spmd.clone, body=%wide.region_50.53_spmd.clone.sunk | while | flops 255886080 | bytes 13063975 | solution.py:327
  1124.4 106.1 %reduce-scatter.12.cloned.1.call-done = bf16[256,384]{1,0:T(8,128)(2,1)} async-done(((bf16[4096,384]{1,0:T(8,128)(2,1)}), bf16[256,384]{1,0:T(8,128)(2,1)}) %reduce-scatter.12.cloned.1.call-update) | async-done | bytes 196624 | tf_op jit(solution)/shard_map/reduce_scatter | solution.py:332
  1253.6 32.2 %all-reduce.20.cloned.1.call-done = (bf16[256,768]{1,0:T(8,128)(2,1)}, bf16[2,256,768]{2,1,0:T(8,128)(2,1)}) async-done(((bf16[256,768]{1,0:T(8,128)(2,1)}, bf16[2,256,768]{2,1,0:T(8,128)(2,1)}), (bf16[256,768]{1,0:T(8,128)(2,1)}, bf16[2,256,768]{2,1,0:T(8,128)(2,1)})) %all-reduce.20.cloned.1.call-update) | async-done | bytes 1179664 | tf_op jit(solution)/shard_map/psum | solution.py:210
  1289.8 51.9 %all-reduce.1 = (f32[1,576]{1,0:T(1,128)}, f32[1,768]{1,0:T(1,128)}, f32[1,768]{1,0:T(1,128)}, f32[1,2,768]{2,1,0:T(2,128)}, f32[1,2,768]{2,1,0:T(2,128)}) all-reduce(f32[1,576]{1,0:T(1,128)} %broadcast_in_dim.273, f32[1,768]{1,0:T(1,128)} %broadcast_in_dim.276, ...), channel_id=1, replica_groups=mesh['section'=2,'ctx'=16,'tp'=4] {'ctx'}, use_global_device_ids=true, to_apply=%region_64.65 | all-reduce | flops 5184 | bytes 41472 | tf_op jit(solution)/shard_map/psum | solution.py:401
  1350.5 28.8 %all-reduce.18.cloned.1.call-done = bf16[768,1344]{0,1:T(8,128)(2,1)} async-done(((bf16[768,1344]{0,1:T(8,128)(2,1)}), bf16[768,1344]{0,1:T(8,128)(2,1)}) %all-reduce.18.cloned.1.call-update) | async-done | bytes 2064400
  (863 shorter events, 570.2 us)
Async XLA Ops:
  7.2 49.7 %all-gather.18.cloned.1.call-start = ((), (), s32[]{:S(2)}) async-start(), calls=%async_computation.4 | async-start | bytes 2297856 | tf_op jit(solution)/shard_map/all_gather | solution.py:129
  8.9 103.0 %all-gather.20.cloned.1.call-start = ((), (), s32[]{:S(2)}) async-start(), calls=%async_computation.5 | async-start | bytes 3342336 | tf_op jit(solution)/shard_map/all_gather | solution.py:194
  11.8 200.4 %copy-start.68 = (f32[256,16]{0,1:T(8,128)}, f32[256,16]{0,1:T(8,128)S(1)}, u32[]{:S(2)}) copy-start(f32[256,16]{0,1:T(8,128)S(1)} %get-tuple-element.1143) | copy-start | bytes 49156
  11.8 220.9 %copy-start.56 = (f32[768]{0:T(1024)}, f32[768]{0:T(1024)S(1)}, u32[]{:S(2)}) copy-start(f32[768]{0:T(1024)S(1)} %get-tuple-element.1141) | copy-start | bytes 9220
  59.8 98.0 %all-gather.22.cloned.1.call-start = ((), (), s32[]{:S(2)}) async-start(), calls=%async_computation.6 | async-start | bytes 1671168 | tf_op jit(solution)/shard_map/all_gather | solution.py:209
  60.6 142.6 %all-reduce.10.cloned.1.call-start = ((), (), s32[]{:S(2)}) async-start(), calls=%async_computation.7 | async-start | bytes 786432 | tf_op jit(solution)/shard_map/psum | solution.py:210
  162.1 102.3 %all-gather.24.cloned.1.call-start = ((), (), s32[]{:S(2)}) async-start(), calls=%async_computation.8 | async-start | bytes 3342336 | tf_op jit(solution)/shard_map/all_gather | solution.py:194
  204.3 5.3 collective-permute-start
  213.1 122.7 %all-reduce.12.cloned.1.call-start = ((), (), s32[]{:S(2)}) async-start(), calls=%async_computation.9 | async-start | bytes 786432 | tf_op jit(solution)/shard_map/psum | solution.py:210
  294.6 103.4 %all-gather.28.cloned.1.call-start = ((), (), s32[]{:S(2)}) async-start(), calls=%async_computation.16 | async-start | bytes 3342336 | tf_op jit(solution)/shard_map/all_gather | solution.py:261
  336.9 5.3 collective-permute-start.1
  346.6 105.3 %all-gather.26.cloned.1.call-start = ((), (), s32[]{:S(2)}) async-start(), calls=%async_computation.10 | async-start | bytes 3342336 | tf_op jit(solution)/shard_map/all_gather | solution.py:194
  347.4 270.4 %reduce-scatter.8.cloned.1.call-start = ((), (), s32[]{:S(2)}) async-start(), calls=%async_computation.11 | async-start | bytes 3342336 | tf_op jit(solution)/shard_map/reduce_scatter | solution.py:332
  516.3 152.4 %all-reduce.14.cloned.1.call-start = ((), (), s32[]{:S(2)}) async-start(), calls=%async_computation.12 | async-start | bytes 1572864 | tf_op jit(solution)/shard_map/psum | solution.py:359
  623.7 100.8 %all-gather.30.cloned.1.call-start = ((), (), s32[]{:S(2)}) async-start(), calls=%async_computation.17 | async-start | bytes 3342336 | tf_op jit(solution)/shard_map/all_gather | solution.py:261
  624.4 299.5 %reduce-scatter.10.cloned.1.call-start = ((), (), s32[]{:S(2)}) async-start(), calls=%async_computation.13 | async-start | bytes 3342336 | tf_op jit(solution)/shard_map/reduce_scatter | solution.py:332
  673.5 60.4 %collective-permute-start.2 = (bf16[256,768]{1,0:T(8,128)(2,1)}, bf16[256,768]{1,0:T(8,128)(2,1)}, u32[]{:S(2)}, u32[]{:S(2)}) collective-permute-start(bf16[256,768]{1,0:T(8,128)(2,1)} %fusion.142), channel_id=1, source_target_pairs={{64,0},{65,1},{66,2},{67,3},{68,4},{69,5},{70,6},{71,7},{72,8},{73... | collective-permute-start | bytes 1179656 | tf_op jit(solution)/shard_map/ppermute | solution.py:15
  786.5 193.1 %all-reduce.16.cloned.1.call-start = ((), (), s32[]{:S(2)}) async-start(), calls=%async_computation.14 | async-start | bytes 1572864 | tf_op jit(solution)/shard_map/psum | solution.py:359
  934.5 100.7 %all-gather.32.cloned.1.call-start = ((), (), s32[]{:S(2)}) async-start(), calls=%async_computation.18 | async-start | bytes 3342336 | tf_op jit(solution)/shard_map/all_gather | solution.py:261
  935.1 187.4 %reduce-scatter.14.cloned.1.call-start = ((), (), s32[]{:S(2)}) async-start(), calls=%async_computation.19 | async-start | bytes 1671168
  983.8 5.6 collective-permute-start.3
  996.3 234.3 %reduce-scatter.12.cloned.1.call-start = ((), (), s32[]{:S(2)}) async-start(), calls=%async_computation.15 | async-start | bytes 3342336 | tf_op jit(solution)/shard_map/reduce_scatter | solution.py:332
  1094.5 191.3 %all-reduce.20.cloned.1.call-start = ((), (), s32[]{:S(2)}) async-start(), calls=%async_computation.21 | async-start | bytes 2359296 | tf_op jit(solution)/shard_map/psum | solution.py:210
  1237.9 141.4 %all-reduce.18.cloned.1.call-start = ((), (), s32[]{:S(2)}) async-start(), calls=%async_computation.20 | async-start | bytes 4128768
  (158 other events, 2793.2 us)
Sparse Core Ops, SparseCore 0:
  10.8 46.0 all-gather.17
  59.9 51.9 all-gather.19
  114.6 43.1 all-gather.21
  162.2 40.9 all-reduce.9
  213.2 51.0 all-gather.23
  294.7 40.9 all-reduce.11
  346.8 51.2 all-gather.27
  400.2 51.7 all-gather.25
  516.5 101.2 reduce-scatter.7
  623.8 44.8 all-reduce.13
  670.8 53.6 all-gather.29
  786.6 137.2 reduce-scatter.9
  934.7 44.8 all-reduce.15
  981.6 53.6 all-gather.31
  1038.3 71.5 reduce-scatter.13
  1113.0 117.4 reduce-scatter.11
  1238.0 47.7 all-reduce.19
  1289.0 90.2 all-reduce.17
where the time goes:
time: 1410 us; the launch traced here: 1390 us
  waiting for transfers between devices  783 us (56%)
  blocking collectives  161 us (11%)
  local copies, waits for them, and re-layouts  153 us (11%)
  matrix products  132 us (9%)
  other arithmetic  114 us (8%)
  between operations  17.9 us (1%)
  loops' own time  16.6 us (1%)
    reduce_scatter x3, waiting for transfers between devices, per_device(): lax.psum_scatter(grad_kv.reshape(seq_length, 2 * head_cols).astype(jnp.bf...  329 us
    psum x3, waiting for transfers between devices, per_device(): lax.psum(branches.astype(jnp.bfloat16), 'tp').astype(jnp.float32)  114 us
    all_gather x3, waiting for transfers between devices, per_device(): lax.all_gather(forward_keyval, 'ctx', axis=0, tiled=True)  108 us
    psum x2, waiting for transfers between devices, per_device(): lax.psum(norm_terms.astype(jnp.bfloat16), 'tp').astype(jnp.float32)  80.3 us
    all_gather x3, blocking collectives, per_device(): whole_seg = lax.all_gather(backward_seg_ids, 'ctx', axis=0, tiled=True)  55 us
    all_gather x3, blocking collectives, per_device(): lax.all_gather(seg_ids, 'ctx', axis=0, tiled=True)  53.6 us
    psum x1, blocking collectives, per_device(): lax.psum(small_total, 'ctx')  51.9 us
    all_gather x3, waiting for transfers between devices, per_device(): whole_kv = lax.all_gather(keyval, 'ctx', axis=0, tiled=True)  49.9 us
  transfers between devices with their start and end apart: 22, of which 20 were waited for; matrix products, arithmetic and copies ran while one was open for 15% of the time, Pallas kernels for 0%

commit v1 on v0

v1 whole, which is shorter than its diff:
```python
import functools

import jax
import jax.numpy as jnp
from jax import lax
from jax.experimental import pallas as pl
from jax.experimental.pallas import tpu as pltpu
from jax.sharding import PartitionSpec as P

HEAD_DIM = 64
ROT = 16
BLOCKS = 9
CHIPS = 16
F32 = jnp.float32
BF16 = jnp.bfloat16
FAR = -1e30


def batch_of(chip):
    return (chip ^ (chip >> 1)) & 1


def dot(left, right):
    return jnp.dot(left, right, preferred_element_type=F32)


def dot_last(left, right):
    return lax.dot_general(left, right, (((1,), (1,)), ((), ())), preferred_element_type=F32)


def dot_first(left, right):
    return lax.dot_general(left, right, (((0,), (0,)), ((), ())), preferred_element_type=F32)


def moved(value, target):
    pairs = []
    for core in range(2):
        for chip in range(CHIPS):
            place = target(core, chip)
            if place is not None:
                pairs.append((core * CHIPS + chip, place[0] * CHIPS + place[1]))
    return lax.ppermute(value, ("section", "ctx"), pairs)


def swapped(value):
    return lax.ppermute(value, "section", [(0, 1), (1, 0)])


def chip_at(index, batch):
    low = 2 * index
    return low if batch_of(low) == batch else low + 1


def shifted(value, steps):
    def target(core, chip):
        index = chip // 2 + steps
        return (core, chip_at(index, batch_of(chip))) if 0 <= index < CHIPS // 2 else None

    return moved(value, target)


def to_home(value):
    return moved(value, lambda core, chip: (batch_of(chip), (chip & ~1) + core))


def from_home(value):
    return moved(value, lambda core, chip: (core, chip ^ 1) if chip % 2 == core else None)


def source(g_ref, r_ref, block):
    ref = g_ref if block % 2 == 0 else r_ref
    return ref, slice((block // 2) * 256, (block // 2) * 256 + 256)


def attend_kernel(q_ref, g_ref, r_ref, qs_ref, ks_ref, o_ref, l_ref, bias_ref, s_ref):
    tile = (256, 256)
    for block in range(BLOCKS):
        cols = slice(block * 256, block * 256 + 256)
        allowed = qs_ref[...] == ks_ref[:, cols]
        if block == BLOCKS - 1:
            rows_of = lax.broadcasted_iota(jnp.int32, tile, 0)
            allowed = allowed & (lax.broadcasted_iota(jnp.int32, tile, 1) <= rows_of)
        bias_ref[:, cols] = jnp.where(allowed, 0.0, FAR)
    heads = q_ref.shape[1] // HEAD_DIM
    for head in range(heads):
        span = slice(head * HEAD_DIM, head * HEAD_DIM + HEAD_DIM)
        vspan = slice((heads + head) * HEAD_DIM, (heads + head) * HEAD_DIM + HEAD_DIM)
        query = q_ref[:, span]
        top = None
        for block in range(BLOCKS):
            cols = slice(block * 256, block * 256 + 256)
            ref, rows = source(g_ref, r_ref, block)
            scores = dot_last(query, ref[rows, span]) + bias_ref[:, cols]
            s_ref[:, cols] = scores
            top = scores if top is None else jnp.maximum(top, scores)
        top = jnp.max(top, axis=1, keepdims=True)
        total = jnp.zeros(tile, F32)
        mixed = jnp.zeros((256, HEAD_DIM), F32)
        for block in range(BLOCKS):
            cols = slice(block * 256, block * 256 + 256)
            ref, rows = source(g_ref, r_ref, block)
            weights = jnp.exp(s_ref[:, cols] - top)
            total = total + weights
            mixed = mixed + dot(weights.astype(BF16), ref[rows, vspan])
        total = jnp.sum(total, axis=1, keepdims=True)
        o_ref[:, span] = mixed / total
        l_ref[:, head : head + 1] = top + jnp.log(total)


def attend_back_kernel(
    q_ref, g_ref, r_ref, do_ref, lse_ref, delta_ref, qs_ref, ks_ref, dq_ref, dg_ref, dr_ref, bias_ref
):
    tile = (256, 256)
    for block in range(BLOCKS):
        rows = slice(block * 256, block * 256 + 256)
        allowed = ks_ref[rows, :] == qs_ref[...]
        if block == BLOCKS - 1:
            keys_of = lax.broadcasted_iota(jnp.int32, tile, 0)
            allowed = allowed & (keys_of <= lax.broadcasted_iota(jnp.int32, tile, 1))
        bias_ref[rows, :] = jnp.where(allowed, 0.0, FAR)
    heads = q_ref.shape[1] // HEAD_DIM
    for head in range(heads):
        span = slice(head * HEAD_DIM, head * HEAD_DIM + HEAD_DIM)
        vspan = slice((heads + head) * HEAD_DIM, (heads + head) * HEAD_DIM + HEAD_DIM)
        query = q_ref[:, span]
        grad_out = do_ref[:, span]
        lse = lse_ref[head : head + 1, :]
        delta = delta_ref[head : head + 1, :]
        grad_query = jnp.zeros((HEAD_DIM, 256), F32)
        for block in range(BLOCKS):
            ref, rows = source(g_ref, r_ref, block)
            out = dg_ref if block % 2 == 0 else dr_ref
            keys = ref[rows, span]
            scores = dot_last(keys, query) + bias_ref[block * 256 : block * 256 + 256, :]
            probs = jnp.exp(scores - lse)
            grad_probs = dot_last(ref[rows, vspan], grad_out)
            grad_scores = (probs * (grad_probs - delta)).astype(BF16)
            out[rows, span] = dot(grad_scores, query).astype(BF16)
            out[rows, vspan] = dot(probs.astype(BF16), grad_out).astype(BF16)
            grad_query = grad_query + dot_first(keys, grad_scores)
        dq_ref[span, :] = grad_query * (HEAD_DIM**-0.5)


def in_vmem(count):
    return [pl.BlockSpec(memory_space=pltpu.VMEM)] * count


def attend(query, g, r, qs, ks):
    return pl.pallas_call(
        attend_kernel,
        out_shape=(
            jax.ShapeDtypeStruct((256, query.shape[1]), F32),
            jax.ShapeDtypeStruct((256, 128), F32),
        ),
        in_specs=in_vmem(5),
        out_specs=tuple(in_vmem(2)),
        scratch_shapes=[pltpu.VMEM((256, BLOCKS * 256), F32), pltpu.VMEM((256, BLOCKS * 256), F32)],
        compiler_params=pltpu.CompilerParams(vmem_limit_bytes=40 * 1024 * 1024),
        cost_estimate=pl.CostEstimate(
            flops=2_000_000_000, bytes_accessed=3_000_000, transcendentals=1_800_000
        ),
    )(query, g, r, qs, ks)


def attend_back(query, g, r, grad_out, lse, delta, qs, ks):
    return pl.pallas_call(
        attend_back_kernel,
        out_shape=(
            jax.ShapeDtypeStruct((query.shape[1], 256), F32),
            jax.ShapeDtypeStruct(g.shape, BF16),
            jax.ShapeDtypeStruct(r.shape, BF16),
        ),
        in_specs=in_vmem(8),
        out_specs=tuple(in_vmem(3)),
        scratch_shapes=[pltpu.VMEM((BLOCKS * 256, 256), F32)],
        compiler_params=pltpu.CompilerParams(vmem_limit_bytes=40 * 1024 * 1024),
        cost_estimate=pl.CostEstimate(
            flops=6_000_000_000, bytes_accessed=6_000_000, transcendentals=1_800_000
        ),
    )(query, g, r, grad_out, lse, delta, qs, ks)


def rotary_tables(first, count, heads):
    frequency = jnp.exp(-(jnp.arange(ROT // 2, dtype=F32) * (2.0 / ROT)) * jnp.log(10000.0))
    places = (first + jnp.arange(count, dtype=jnp.int32)).astype(F32)
    angles = places[:, None] * frequency[None, :]
    cosine, sine = jnp.cos(angles), jnp.sin(angles)
    ones = jnp.ones((count, HEAD_DIM - ROT), F32)
    zeros = jnp.zeros((count, HEAD_DIM - ROT), F32)
    cos_row = jnp.concatenate([cosine, cosine, ones], 1)
    sin_row = jnp.concatenate([-sine, sine, zeros], 1)
    return jnp.tile(cos_row, (1, heads)), jnp.tile(sin_row, (1, heads))


def turned(values):
    half = ROT // 2
    up = jnp.concatenate([values[:, half:], values[:, :half]], 1)
    down = jnp.concatenate([values[:, -half:], values[:, :-half]], 1)
    low = (lax.broadcasted_iota(jnp.int32, values.shape, 1) % HEAD_DIM) < half
    return jnp.where(low, up, down)


def rotate(values, tables, sign):
    return values * tables[0] + turned(values) * (sign * tables[1])


def gelu(values):
    return 0.5 * values * (1.0 + lax.erf(values * 0.7071067811865476))


def gelu_slope(values):
    return (
        0.5 * (1.0 + lax.erf(values * 0.7071067811865476))
        + values * jnp.exp(-0.5 * values * values) * 0.3989422804014327
    )


def tp_scatter(values):
    parts = values.astype(BF16).reshape(4, 64, values.shape[1])
    parts = lax.all_to_all(parts, "tp", 0, 0, tiled=True)
    return jnp.sum(parts.astype(F32), axis=0)


def tp_gather(rows):
    spread = jnp.broadcast_to(rows[None], (4,) + rows.shape)
    return lax.all_to_all(spread, "tp", 0, 0, tiled=True)


def per_device(
    inputs,
    cotangent,
    segments,
    w_qkv,
    b_qkv,
    w_out,
    w_up,
    b_up,
    w_down,
    b_out,
    norm_gain,
    norm_bias,
):
    core = lax.axis_index("section")
    chip = lax.axis_index("ctx")
    rank = lax.axis_index("tp")
    batch = batch_of(chip)
    shard = (chip & ~1) + core
    at_home = (chip % 2) == core
    tokens, width = inputs.shape[1], inputs.shape[2]
    qkv_cols, up_cols, att_cols = w_qkv.shape[2], w_up.shape[2], w_out.shape[2]
    heads = att_cols // HEAD_DIM
    part_rows = w_qkv.shape[1]

    def by_core(first, second):
        return jnp.where(core == 0, first, second)

    def of_layers(mine):
        other = swapped(mine)
        return by_core(mine, other), by_core(other, mine)

    def to_parts(cols):
        lead = cols.shape[:-1]
        return jnp.swapaxes(cols.reshape(lead + (heads, 3, HEAD_DIM)), -3, -2).reshape(cols.shape)

    def to_heads(cols):
        lead = cols.shape[:-1]
        return jnp.swapaxes(cols.reshape(lead + (3, heads, HEAD_DIM)), -3, -2).reshape(cols.shape)

    rows_at = rank * (tokens // 4)

    def own_rows(values):
        return lax.dynamic_slice_in_dim(values, rows_at, tokens // 4, 0)

    away_x = from_home(jnp.where(batch == 0, inputs[1], inputs[0]))
    first_x = jnp.where(at_home, jnp.where(batch == 0, inputs[0], inputs[1]), away_x)
    away_g = from_home(jnp.where(batch == 0, cotangent[1], cotangent[0]))
    last_g = jnp.where(at_home, jnp.where(batch == 0, cotangent[0], cotangent[1]), away_g)

    seg_row = jnp.concatenate(
        [segments.reshape(1, 2 * tokens).astype(BF16), jnp.zeros((1, qkv_cols - 2 * tokens), BF16)], 1
    )
    piece = jnp.concatenate(
        [to_parts(w_qkv[0]), seg_row, jnp.zeros((7, qkv_cols), BF16)], 0
    )
    spread = jnp.broadcast_to(piece[None], (CHIPS,) + piece.shape)
    spread = lax.all_to_all(spread, "ctx", 0, 0, tiled=True)
    weight_in = of_layers(spread[:, :part_rows].reshape(width, qkv_cols))
    all_segs = spread[:, part_rows, : 2 * tokens].astype(F32).reshape(CHIPS, 2, tokens)
    all_segs = jnp.where(batch == 0, all_segs[:, 0], all_segs[:, 1]).reshape(CHIPS * tokens)
    all_segs = jnp.concatenate([jnp.full(((BLOCKS - 1) * tokens,), -1.0, F32), all_segs])
    key_segs = lax.dynamic_slice_in_dim(all_segs, shard * tokens, BLOCKS * tokens)
    own_segs = key_segs[(BLOCKS - 1) * tokens :]

    rest = jnp.concatenate([w_up[0], w_out[0], w_down[0]], 1)
    rest = lax.all_gather(rest, "ctx", axis=0, tiled=True)
    small = jnp.concatenate(
        [
            jnp.concatenate([to_parts(b_qkv[0]), jnp.zeros((width - qkv_cols,), BF16)])[None],
            b_up,
            b_out,
            norm_gain[0],
            norm_bias[0],
            jnp.zeros((1, width), BF16),
        ],
        0,
    )
    smalls = of_layers(small)
    tables = rotary_tables(shard * tokens, tokens, heads)
    scale = HEAD_DIM**-0.5

    def forward(layer, x, rest):
        vectors = smalls[layer].astype(F32)
        bias_in, bias_up, bias_out = vectors[0, :qkv_cols], vectors[1], vectors[2]
        values = x.astype(F32)
        center = values - jnp.mean(values, axis=-1, keepdims=True)
        inverse = lax.rsqrt(jnp.mean(center * center, axis=-1, keepdims=True) + 1e-05)
        normed = center * inverse
        first_in = (normed * vectors[3] + vectors[5]).astype(BF16)
        second_in = (normed * vectors[4] + vectors[6]).astype(BF16)
        packed = dot(first_in, weight_in[layer]) + bias_in
        query = (rotate(packed[:, :att_cols], tables, 1.0).astype(BF16) * scale).astype(BF16)
        key = rotate(packed[:, att_cols : 2 * att_cols], tables, 1.0).astype(BF16)
        keyval = jnp.concatenate([key, packed[:, 2 * att_cols :].astype(BF16)], 1)
        g = jnp.concatenate([shifted(keyval, steps) for steps in (4, 3, 2, 1)] + [keyval], 0)
        r = swapped(by_core(g[tokens:], g[:-tokens]))
        if layer == 0:
            g, rest = lax.optimization_barrier((g, rest))
            rest = of_layers(rest)
        weight_up = rest[layer][:, :up_cols]
        weight_out = rest[layer][:, up_cols : up_cols + att_cols]
        weight_down = rest[layer][:, up_cols + att_cols :]
        mixed, lse = attend(query, g, r, own_segs[:, None], key_segs[None, :])
        hidden_pre = dot(second_in, weight_up) + bias_up
        hidden = gelu(hidden_pre).astype(BF16)
        mixed_low = mixed.astype(BF16)
        branches = dot_last(mixed_low, weight_out) + dot_last(hidden, weight_down)
        total = tp_scatter(branches)
        result = (own_rows(x).astype(F32) + total + bias_out).astype(BF16)
        result = tp_gather(result).reshape(tokens, width)
        kept = (normed, inverse, first_in, second_in, query, g, r, mixed, lse, hidden_pre, hidden)
        return result, kept, rest

    def backward(layer, grad_low, kept):
        normed, inverse, first_in, second_in, query, g, r, mixed, lse, hidden_pre, hidden = kept
        vectors = smalls[layer].astype(F32)
        weight_up = rest[layer][:, :up_cols]
        weight_out = rest[layer][:, up_cols : up_cols + att_cols]
        weight_down = rest[layer][:, up_cols + att_cols :]
        grad_mixed = dot(grad_low, weight_out).astype(BF16)
        delta = jnp.sum(
            (grad_mixed.astype(F32) * mixed).reshape(tokens, heads, HEAD_DIM), axis=-1
        )
        grad_pre = (dot(grad_low, weight_down) * gelu_slope(hidden_pre)).astype(BF16)
        grad_query, dg, dr = attend_back(
            query,
            g,
            r,
            grad_mixed,
            lse[:, :heads].T,
            delta.T,
            own_segs[None, :],
            key_segs[:, None],
        )
        partner = swapped(dr).astype(F32)
        zero = jnp.zeros((tokens, 2 * att_cols), F32)
        partner = by_core(
            jnp.concatenate([zero, partner], 0), jnp.concatenate([partner, zero], 0)
        )
        dg = dg.astype(F32) + partner
        sent = dg.astype(BF16)
        grad_keyval = dg[4 * tokens :]
        for slot in range(4):
            part = sent[slot * tokens : (slot + 1) * tokens]
            grad_keyval = grad_keyval + shifted(part, slot - 4).astype(F32)
        grad_packed = jnp.concatenate(
            [
                rotate(grad_query.T, tables, -1.0),
                rotate(grad_keyval[:, :att_cols], tables, -1.0),
                grad_keyval[:, att_cols:],
            ],
            1,
        ).astype(BF16)
        first_grad = dot_last(grad_packed, weight_in[layer])
        second_grad = dot_last(grad_pre, weight_up)
        scaled = tp_scatter(first_grad * vectors[3] + second_grad * vectors[4])
        rows_normed = own_rows(normed)
        grad_input = own_rows(grad_low).astype(F32) + own_rows(inverse) * (
            scaled
            - jnp.mean(scaled, axis=-1, keepdims=True)
            - rows_normed * jnp.mean(scaled * rows_normed, axis=-1, keepdims=True)
        )
        bias_in_grad = jnp.sum(grad_packed.astype(F32), axis=0)
        sums = jnp.stack(
            [
                jnp.concatenate([bias_in_grad, jnp.zeros((width - qkv_cols,), F32)]),
                jnp.sum(grad_pre.astype(F32), axis=0),
                jnp.sum(grad_low.astype(F32), axis=0),
                jnp.sum(first_grad * normed, axis=0),
                jnp.sum(second_grad * normed, axis=0),
                jnp.sum(first_grad, axis=0),
                jnp.sum(second_grad, axis=0),
                jnp.zeros((width,), F32),
            ]
        )
        weight_grad = jnp.concatenate(
            [
                dot_first(first_in, grad_packed).astype(BF16),
                dot_first(second_in, grad_pre).astype(BF16),
                dot_first(grad_low, mixed.astype(BF16)).astype(BF16),
                dot_first(grad_low, hidden).astype(BF16),
            ],
            1,
        )
        return grad_input, sums, weight_grad

    def core_halves(weight_grad):
        halves = weight_grad.reshape(CHIPS, 2, part_rows // 2, weight_grad.shape[1])
        got = swapped(by_core(halves[:, 1], halves[:, 0]))
        return (by_core(halves[:, 0], halves[:, 1]).astype(F32) + got.astype(F32)).astype(BF16)

    first_y, first_kept, rest = forward(0, first_x, rest)
    last_y, last_kept, rest = forward(1, first_y, rest)
    hidden_home = to_home(jnp.stack([first_y, last_y]))

    def weight_sums(weight_grad, sums):
        halves = core_halves(weight_grad)
        cols = weight_grad.shape[1]
        sums = sums + swapped(sums)
        high = sums.astype(BF16)
        fine = (sums - high.astype(F32)).astype(BF16)
        extra = jnp.concatenate([high, fine], 0).reshape(-1)
        extra = jnp.concatenate([extra, jnp.zeros((8 * cols - extra.shape[0],), BF16)])
        extra = jnp.broadcast_to(extra.reshape(1, 8, cols), (CHIPS, 8, cols))
        parcel = lax.all_to_all(jnp.concatenate([halves, extra], 1), "ctx", 0, 0, tiled=True)
        parcel = jnp.sum(parcel.astype(F32), axis=0)
        half = part_rows // 2
        both = parcel[half:].reshape(-1)[: 16 * width].reshape(2, 8, width)
        return parcel[:half], both[0] + both[1]

    top_grad, top_sums, top_weight = backward(1, last_g, last_kept)
    top_home = tp_gather(top_grad).reshape(tokens, width)
    middle = top_home.astype(BF16)
    top_home = to_home(top_home)
    top_weight, top_sums = weight_sums(top_weight, top_sums)

    low_grad, low_sums, low_weight = backward(0, middle, first_kept)
    low_home = to_home(low_grad)
    low_weight, low_sums = weight_sums(low_weight, low_sums)

    sums = by_core(low_sums, top_sums)
    final = jnp.concatenate([low_home, sums[3:7], jnp.zeros((4, width), F32)], 0)
    final = tp_gather(final)
    norms = jnp.sum(final[:, tokens // 4 : tokens // 4 + 4], axis=0)
    low_home = final[:, : tokens // 4].reshape(tokens, width)

    def two_batches(layers):
        mine = by_core(layers[0], layers[1])
        got = swapped(by_core(layers[1], layers[0]))
        return jnp.stack([by_core(mine, got), by_core(got, mine)])

    hidden_out = two_batches(hidden_home)[None]
    input_grad = two_batches((low_home, top_home))[None]
    mine = by_core(low_weight, top_weight)
    got = swapped(by_core(top_weight, low_weight))
    weight = jnp.concatenate([by_core(mine, got), by_core(got, mine)], 0)
    up_end = qkv_cols + up_cols
    out_end = up_end + att_cols
    return (
        hidden_out,
        input_grad,
        to_heads(weight[:, :qkv_cols])[None],
        to_heads(sums[0, :qkv_cols])[None],
        weight[:, up_end:out_end][None],
        weight[:, qkv_cols:up_end][None],
        sums[1][None],
        weight[:, out_end:][None],
        sums[2][None],
        norms[:2][None],
        norms[2:][None],
    )


def solution(mesh):
    placed = (
        P(None, "ctx", None),
        P(None, "ctx", None),
        P(None, "ctx"),
        P("section", "ctx", "tp"),
        P("section", "tp"),
        P("section", "ctx", "tp"),
        P("section", "ctx", "tp"),
        P("section", "tp"),
        P("section", "ctx", "tp"),
        P("section", None),
        P("section", None, None),
        P("section", None, None),
    )
    return jax.shard_map(
        per_device,
        mesh=mesh,
        in_specs=placed,
        out_specs=(
            P("section", None, "ctx", None),
            P("section", None, "ctx", None),
            P("section", "ctx", "tp"),
            P("section", "tp"),
            P("section", "ctx", "tp"),
            P("section", "ctx", "tp"),
            P("section", "tp"),
            P("section", "ctx", "tp"),
            P("section", None),
            P("section", None, None),
            P("section", None, None),
        ),
        check_vma=False,
    )
```

time: 1410 us -> 459 us (0.33)
  waiting for transfers between devices: 783 us -> 110 us
  blocking collectives: 161 us -> 0 us
  starting transfers between devices: 13.3 us -> 138 us
  matrix products: 132 us -> 35.9 us
  local copies, waits for them, and re-layouts: 153 us -> 63.2 us
  other arithmetic: 114 us -> 65.3 us
  Pallas kernels: 0 us -> 21.6 us
  loops' own time: 16.6 us -> 0 us
    reduce_scatter x3 -> x0, waiting for transfers between devices: 329 us -> none  [per_device(): lax.psum_scatter(grad_kv.reshape(seq_length, 2 * head_cols).astype(jnp.bf...]
    all_gather x8 -> x1, waiting for transfers between devices: 220 us -> 0.02 us  [per_device(): rest = lax.all_gather(rest, 'ctx', axis=0, tiled=True)]
    psum x5 -> x0, waiting for transfers between devices: 195 us -> none  [the longest x3 114 us: per_device(): lax.psum(branches.astype(jnp.bfloat16), 'tp').astype(jnp.float32)]
    all_gather x6 -> x0, blocking collectives: 109 us -> none  [the longest x3 55 us: per_device(): whole_seg = lax.all_gather(backward_seg_ids, 'ctx', axis=0, tiled=True)]
    dot_general x48 -> x8, matrix products: 96 us -> 13.1 us  [dot(): return jnp.dot(left, right, preferred_element_type=F32)]
    all_to_all x0 -> x11, waiting for transfers between devices: none -> 65.2 us  [the longest x4 23.8 us: tp_gather(): return lax.all_to_all(spread, 'tp', 0, 0, tiled=True)]
    ppermute x4 -> x35, starting transfers between devices: 11.9 us -> 76.8 us  [the longest x21 56.9 us: moved(): return lax.ppermute(value, ('section', 'ctx'), pairs)]
    all_to_all x0 -> x11, starting transfers between devices: none -> 61.7 us  [the longest x2 20.9 us: weight_sums(): lax.all_to_all(jnp.concatenate([halves, extra], 1), 'ctx', 0, 0, tiled=True)]
  transfers between devices with their start and end apart: 22 -> 47, of which waited for: 20 -> 21; matrix products, arithmetic and copies ran while one was open for 15% -> 27% of each run, Pallas kernels for 0% -> 2%
where the time goes in v1:
time: 459 us; the launch traced here: 451 us
  starting transfers between devices  138 us (30%)
  waiting for transfers between devices  110 us (24%)
  other arithmetic  65.3 us (14%)
  local copies, waits for them, and re-layouts  63.2 us (14%)
  matrix products  35.9 us (8%)
  Pallas kernels  21.6 us (5%)
  between operations  16.3 us (4%)
    ppermute x21, starting transfers between devices, moved(): return lax.ppermute(value, ('section', 'ctx'), pairs)  56.9 us
    ppermute x21, waiting for transfers between devices, moved(): return lax.ppermute(value, ('section', 'ctx'), pairs)  39.6 us
    all_to_all x4, waiting for transfers between devices, tp_gather(): return lax.all_to_all(spread, 'tp', 0, 0, tiled=True)  23.8 us
    all_to_all x2, starting transfers between devices, weight_sums(): lax.all_to_all(jnp.concatenate([halves, extra], 1), 'ctx', 0, 0, tiled=True)  20.9 us
    ppermute x14, starting transfers between devices, swapped(): return lax.ppermute(value, 'section', [(0, 1), (1, 0)])  19.8 us
    all_to_all x4, starting transfers between devices, tp_scatter(): parts = lax.all_to_all(parts, 'tp', 0, 0, tiled=True)  17.1 us
    all_to_all x1, waiting for transfers between devices, per_device(): spread = lax.all_to_all(spread, 'ctx', 0, 0, tiled=True)  16.1 us
    all_to_all x4, starting transfers between devices, tp_gather(): return lax.all_to_all(spread, 'tp', 0, 0, tiled=True)  15.5 us
  transfers between devices with their start and end apart: 47, of which 21 were waited for; matrix products, arithmetic and copies ran while one was open for 27% of the time, Pallas kernels for 2%

profile of v1, /device:TPU:7, one launch (start us, length us, event | category | flops | bytes accessed | tf_op | source)
XLA Modules:
  0.0 450.6 jit_solution(12809556545833152284)
XLA Ops:
  17.7 8.2 %all-to-all-start = ((bf16[16,56,576]{2,1,0:T(8,128)(2,1)}), bf16[16,56,576]{2,1,0:T(8,128)(2,1)S(1)}, u32[]{:S(2)}, u32[]{:S(2)}) async-start(bf16[16,56,576]{2,1,0:T(8,128)(2,1)} %broadcast_in_dim.55), calls=%async_computation | async-start | bytes 2293760 | tf_op jit(solution)/shard_map/all_to_all | solution.py:286
  26.7 16.1 %all-to-all-done = bf16[16,56,576]{2,1,0:T(8,128)(2,1)S(1)} async-done(((bf16[16,56,576]{2,1,0:T(8,128)(2,1)}), bf16[16,56,576]{2,1,0:T(8,128)(2,1)S(1)}, u32[]{:S(2)}, u32[]{:S(2)}) %all-to-all-start) | async-done | bytes 1032224 | tf_op jit(solution)/shard_map/all_to_all | solution.py:286
  69.8 7.9 %collective-permute-done.5 = bf16[256,384]{1,0:T(8,128)(2,1)S(1)} collective-permute-done((bf16[256,384]{1,0:T(8,128)(2,1)S(1)}, bf16[256,384]{1,0:T(8,128)(2,1)S(1)}, u32[]{:S(2)}, u32[]{:S(2)}) %collective-permute-start.5) | collective-permute-done | bytes 196640 | tf_op jit(solution)/shard_map/ppermute | solution.py:42
  78.0 5.0 %copy.174 = bf16[768,1728]{0,1:T(8,128)(2,1)} copy(bf16[768,1728]{1,0:T(8,128)(2,1)} %all-gather.2.cloned.1.call-done) | data formatting | bytes 5308416 | tf_op jit(solution)/shard_map/optimization_barrier | solution.py:327
  92.8 4.6 %copy.175 = bf16[768,1728]{1,0:T(8,128)(2,1)} copy(bf16[768,1728]{0,1:T(8,128)(2,1)} %collective-permute-done.8) | data formatting | bytes 5308416 | tf_op jit(solution)/shard_map/ppermute | solution.py:46
  97.4 4.6 %broadcast_select_fusion = (bf16[768,1728]{1,0:T(8,128)(2,1)}, bf16[768,1728]{1,0:T(8,128)(2,1)S(1)}) fusion(bf16[768,1728]{1,0:T(8,128)(2,1)} %copy.175, bf16[768,1728]{1,0:T(8,128)(2,1)} %all-gather.2.cloned.1.call-done, pred[]{:T(512)S(6)} %eq.17), kind=kLoop, calls=%fused_computation.9 | loop fusion | flops 2654208 | bytes 10616833 | tf_op jit(solution)/shard_map/jit(_where)/select_n | solution.py:255
  105.5 4.9 %all-to-all-start.1 = ((bf16[4,64,768]{2,1,0:T(8,128)(2,1)}), bf16[4,64,768]{2,1,0:T(8,128)(2,1)S(1)}, u32[]{:S(2)}, u32[]{:S(2)}) async-start(bf16[4,64,768]{2,1,0:T(8,128)(2,1)} %bitcast.166), calls=%async_computation.1 | async-start | bytes 786432 | tf_op jit(solution)/shard_map/all_to_all | solution.py:220
  123.1 5.7 %all-to-all-done.2 = bf16[4,64,768]{2,1,0:T(8,128)(2,1)S(1)} async-done(((bf16[4,64,768]{2,1,0:T(8,128)(2,1)}), bf16[4,64,768]{2,1,0:T(8,128)(2,1)S(1)}, u32[]{:S(2)}, u32[]{:S(2)}) %all-to-all-start.2) | async-done | bytes 393248 | tf_op jit(solution)/shard_map/all_to_all | solution.py:226
  134.7 8.8 %collective-permute-start.10 = (bf16[256,384]{1,0:T(8,128)(2,1)}, bf16[256,384]{1,0:T(8,128)(2,1)S(1)}, u32[]{:S(2)}, u32[]{:S(2)}) collective-permute-start(bf16[256,384]{1,0:T(8,128)(2,1)} %pad_maximum_fusion.8), channel_id=1, source_target_pairs={{0,28},{4,24},{8,36},{12,32},{16,44},{20,40},{24,52},{28,48},{32,6... | collective-permute-start | bytes 589832 | tf_op jit(solution)/shard_map/ppermute | solution.py:42
  167.2 7.3 %shard_map.205 = (f32[192,256]{1,0:T(8,128)S(1)}, bf16[1280,384]{1,0:T(8,128)(2,1)S(1)}, bf16[1024,384]{1,0:T(8,128)(2,1)}) custom-call(bf16[256,192]{1,0:T(8,128)(2,1)S(1)} %get-tuple-element.100.q_ref, bf16[1280,384]{1,0:T(8,128)(2,1)S(1)} %copy-done.3, bf16[1024,384]{1,0:T(8,128)(2,1)S(1)} %copy-done.7, bf16[256,192]{1,0:T(8,128)(2,1)S(1)} %get-tuple-element.155.do_ref, ...), custom_call_target="tpu_custom_call" | custom-call | flops 6000000000 | bytes 6000000 | tf_op jit(solution)/shard_map/pallas_call | solution.py:166
  184.4 5.5 %all-to-all-done.3 = bf16[4,64,768]{2,1,0:T(8,128)(2,1)} async-done(((bf16[4,64,768]{2,1,0:T(8,128)(2,1)}), bf16[4,64,768]{2,1,0:T(8,128)(2,1)}, u32[]{:S(2)}, u32[]{:S(2)}) %all-to-all-start.3) | async-done | bytes 393248 | tf_op jit(solution)/shard_map/all_to_all | solution.py:220
  196.6 6.2 %collective-permute-start.21 = (bf16[256,384]{1,0:T(8,128)(2,1)S(1)}, bf16[256,384]{1,0:T(8,128)(2,1)S(1)}, u32[]{:S(2)}, u32[]{:S(2)}) collective-permute-start(bf16[256,384]{1,0:T(8,128)(2,1)S(1)} %get-tuple-element.78), channel_id=1, source_target_pairs={{8,4},{12,0},{16,12},{20,8},{24,20},{28,16},{32,28},{36,24},{40,36... | collective-permute-start | bytes 589832 | tf_op jit(solution)/shard_map/ppermute | solution.py:42
  225.2 5.8 %copy.200 = bf16[768,2304]{1,0:T(8,128)(2,1)} copy(bf16[768,2304]{0,1:T(8,128)(2,1)} %pad_maximum_fusion.1) | data formatting | bytes 7077888 | tf_op jit(solution)/shard_map/concatenate | solution.py:405
  236.6 4.5 all-to-all-start.6
  245.6 7.6 %all-to-all-done.6 = f32[4,64,768]{2,1,0:T(8,128)S(1)} async-done(((f32[4,64,768]{2,1,0:T(8,128)}), f32[4,64,768]{2,1,0:T(8,128)S(1)}, u32[]{:S(2)}, u32[]{:S(2)}) %all-to-all-start.6) | async-done | bytes 786464 | tf_op jit(solution)/shard_map/all_to_all | solution.py:226
  266.4 7.3 %shard_map.206 = (f32[192,256]{1,0:T(8,128)S(1)}, bf16[1280,384]{1,0:T(8,128)(2,1)S(1)}, bf16[1024,384]{1,0:T(8,128)(2,1)}) custom-call(bf16[256,192]{1,0:T(8,128)(2,1)S(1)} %get-tuple-element.101.q_ref, bf16[1280,384]{1,0:T(8,128)(2,1)S(1)} %copy-done.1, bf16[1024,384]{1,0:T(8,128)(2,1)S(1)} %copy-done.5, bf16[256,192]{1,0:T(8,128)(2,1)S(1)} %get-tuple-element.159.do_ref, ...), custom_call_target="tpu_custom_call" | custom-call | flops 6000000000 | bytes 6000000 | tf_op jit(solution)/shard_map/pallas_call | solution.py:166
  287.6 8.0 %collective-permute-done.23 = bf16[256,384]{1,0:T(8,128)(2,1)S(1)} collective-permute-done((bf16[256,384]{1,0:T(8,128)(2,1)S(1)}, bf16[256,384]{1,0:T(8,128)(2,1)S(1)}, u32[]{:S(2)}, u32[]{:S(2)}) %collective-permute-start.23) | collective-permute-done | bytes 196640 | tf_op jit(solution)/shard_map/ppermute | solution.py:42
  316.1 4.5 all-to-all-start.7
  327.6 12.8 %all-to-all-start.9 = ((bf16[16,32,2304]{2,1,0:T(8,128)(2,1)}), bf16[16,32,2304]{2,1,0:T(8,128)(2,1)}, u32[]{:S(2)}, u32[]{:S(2)}) async-start(bf16[16,32,2304]{2,1,0:T(8,128)(2,1)} %pad_maximum_fusion.3), calls=%async_computation.9 | async-start | bytes 4718592 | tf_op jit(solution)/shard_map/all_to_all | solution.py:434
  364.2 4.5 %all-to-all-done.9 = bf16[16,32,2304]{2,1,0:T(8,128)(2,1)} async-done(((bf16[16,32,2304]{2,1,0:T(8,128)(2,1)}), bf16[16,32,2304]{2,1,0:T(8,128)(2,1)}, u32[]{:S(2)}, u32[]{:S(2)}) %all-to-all-start.9) | async-done | bytes 2359328 | tf_op jit(solution)/shard_map/all_to_all | solution.py:434
  368.8 8.1 %all-to-all-start.8 = ((bf16[16,32,2304]{2,1,0:T(8,128)(2,1)}), bf16[16,32,2304]{2,1,0:T(8,128)(2,1)S(1)}, u32[]{:S(2)}, u32[]{:S(2)}) async-start(bf16[16,32,2304]{2,1,0:T(8,128)(2,1)} %pad_maximum_fusion.2), calls=%async_computation.8 | async-start | bytes 4718592 | tf_op jit(solution)/shard_map/all_to_all | solution.py:434
  396.4 8.8 %all-to-all-done.8 = bf16[16,32,2304]{2,1,0:T(8,128)(2,1)S(1)} async-done(((bf16[16,32,2304]{2,1,0:T(8,128)(2,1)}), bf16[16,32,2304]{2,1,0:T(8,128)(2,1)S(1)}, u32[]{:S(2)}, u32[]{:S(2)}) %all-to-all-start.8) | async-done | bytes 2359328 | tf_op jit(solution)/shard_map/all_to_all | solution.py:434
  406.3 8.3 %collective-permute-done.27 = f32[64,768]{1,0:T(8,128)} collective-permute-done((f32[64,768]{1,0:T(8,128)}, f32[64,768]{1,0:T(8,128)}, u32[]{:S(2)}, u32[]{:S(2)}) %collective-permute-start.27) | collective-permute-done | bytes 196640 | tf_op jit(solution)/shard_map/ppermute | solution.py:42
  422.3 10.4 %all-to-all-done.10 = f32[4,72,768]{2,1,0:T(8,128)S(1)} async-done(((f32[4,72,768]{2,1,0:T(8,128)}), f32[4,72,768]{2,1,0:T(8,128)S(1)}, u32[]{:S(2)}, u32[]{:S(2)}) %all-to-all-start.10) | async-done | bytes 884768 | tf_op jit(solution)/shard_map/all_to_all | solution.py:226
  (475 shorter events, 259.1 us)
Async XLA Ops:
  7.2 70.8 %all-gather.2.cloned.1.call-start = ((), (), s32[]{:S(2)}) async-start(), calls=%async_computation.11 | async-start | bytes 2924544 | tf_op jit(solution)/shard_map/all_gather | solution.py:295
  10.2 35.6 %collective-permute-start = (bf16[256,768]{1,0:T(8,128)(2,1)S(1)}, bf16[256,768]{1,0:T(8,128)(2,1)}, u32[]{:S(2)}, u32[]{:S(2)}) collective-permute-start(bf16[256,768]{1,0:T(8,128)(2,1)S(1)} %select_bitcast_fusion.6), channel_id=1, source_target_pairs={{0,4},{8,12},{16,20},{24,28},{32,36},{40,44},{48,52},{56,60},{68,6... | collective-permute-start | bytes 1179656 | tf_op jit(solution)/shard_map/ppermute | solution.py:42
  17.7 25.2 %all-to-all-start = ((bf16[16,56,576]{2,1,0:T(8,128)(2,1)}), bf16[16,56,576]{2,1,0:T(8,128)(2,1)S(1)}, u32[]{:S(2)}, u32[]{:S(2)}) async-start(bf16[16,56,576]{2,1,0:T(8,128)(2,1)} %broadcast_in_dim.55), calls=%async_computation | async-start | bytes 2293760 | tf_op jit(solution)/shard_map/all_to_all | solution.py:286
  53.2 14.7 %collective-permute-start.3 = (bf16[256,384]{1,0:T(8,128)(2,1)S(1)}, bf16[256,384]{1,0:T(8,128)(2,1)S(1)}, u32[]{:S(2)}, u32[]{:S(2)}) collective-permute-start(bf16[256,384]{1,0:T(8,128)(2,1)S(1)} %pad_maximum_fusion.7), channel_id=1, source_target_pairs={{0,32},{4,36},{8,40},{12,44},{16,48},{20,52},{24,56},{28,60},{64,9... | collective-permute-start | bytes 589832 | tf_op jit(solution)/shard_map/ppermute | solution.py:42
  61.2 16.6 %collective-permute-start.5 = (bf16[256,384]{1,0:T(8,128)(2,1)S(1)}, bf16[256,384]{1,0:T(8,128)(2,1)S(1)}, u32[]{:S(2)}, u32[]{:S(2)}) collective-permute-start(bf16[256,384]{1,0:T(8,128)(2,1)S(1)} %pad_maximum_fusion.7), channel_id=1, source_target_pairs={{0,16},{4,20},{8,24},{12,28},{16,32},{20,36},{24,40},{28,44},{32,4... | collective-permute-start | bytes 589832 | tf_op jit(solution)/shard_map/ppermute | solution.py:42
  134.7 19.9 %collective-permute-start.10 = (bf16[256,384]{1,0:T(8,128)(2,1)}, bf16[256,384]{1,0:T(8,128)(2,1)S(1)}, u32[]{:S(2)}, u32[]{:S(2)}) collective-permute-start(bf16[256,384]{1,0:T(8,128)(2,1)} %pad_maximum_fusion.8), channel_id=1, source_target_pairs={{0,28},{4,24},{8,36},{12,32},{16,44},{20,40},{24,52},{28,48},{32,6... | collective-permute-start | bytes 589832 | tf_op jit(solution)/shard_map/ppermute | solution.py:42
  174.5 16.5 %collective-permute-start.17 = (bf16[1024,384]{1,0:T(8,128)(2,1)}, bf16[1024,384]{1,0:T(8,128)(2,1)}, u32[]{:S(2)}, u32[]{:S(2)}) collective-permute-start(bf16[1024,384]{1,0:T(8,128)(2,1)} %get-tuple-element.30), channel_id=1, source_target_pairs={{0,64},{64,0},{1,65},{65,1},{2,66},{66,2},{3,67},{67,3},{4,68},{68... | collective-permute-start | bytes 2359304 | tf_op jit(solution)/shard_map/ppermute | solution.py:46
  195.3 16.2 %collective-permute-start.20 = (bf16[256,384]{1,0:T(8,128)(2,1)S(1)}, bf16[256,384]{1,0:T(8,128)(2,1)S(1)}, u32[]{:S(2)}, u32[]{:S(2)}) collective-permute-start(bf16[256,384]{1,0:T(8,128)(2,1)S(1)} %get-tuple-element.79), channel_id=1, source_target_pairs={{16,0},{20,4},{24,8},{28,12},{32,16},{36,20},{40,24},{44,28},{48,3... | collective-permute-start | bytes 589832 | tf_op jit(solution)/shard_map/ppermute | solution.py:42
  196.6 14.9 %collective-permute-start.21 = (bf16[256,384]{1,0:T(8,128)(2,1)S(1)}, bf16[256,384]{1,0:T(8,128)(2,1)S(1)}, u32[]{:S(2)}, u32[]{:S(2)}) collective-permute-start(bf16[256,384]{1,0:T(8,128)(2,1)S(1)} %get-tuple-element.78), channel_id=1, source_target_pairs={{8,4},{12,0},{16,12},{20,8},{24,20},{28,16},{32,28},{36,24},{40,36... | collective-permute-start | bytes 589832 | tf_op jit(solution)/shard_map/ppermute | solution.py:42
  218.3 15.0 %all-to-all-start.5 = ((bf16[4,64,768]{2,1,0:T(8,128)(2,1)}), bf16[4,64,768]{2,1,0:T(8,128)(2,1)S(1)}, u32[]{:S(2)}, u32[]{:S(2)}) async-start(bf16[4,64,768]{2,1,0:T(8,128)(2,1)} %bitcast.174), calls=%async_computation.5 | async-start | bytes 786432 | tf_op jit(solution)/shard_map/all_to_all | solution.py:220
  236.6 16.6 %all-to-all-start.6 = ((f32[4,64,768]{2,1,0:T(8,128)}), f32[4,64,768]{2,1,0:T(8,128)S(1)}, u32[]{:S(2)}, u32[]{:S(2)}) async-start(f32[4,64,768]{2,1,0:T(8,128)} %broadcast_in_dim.125), calls=%async_computation.6 | async-start | bytes 1572864 | tf_op jit(solution)/shard_map/all_to_all | solution.py:226
  244.5 65.2 %collective-permute-start.30 = (bf16[16,24,2304]{2,1,0:T(8,128)(2,1)}, bf16[16,24,2304]{2,1,0:T(8,128)(2,1)}, u32[]{:S(2)}, u32[]{:S(2)}) collective-permute-start(bf16[16,24,2304]{2,1,0:T(8,128)(2,1)} %select_bitcast_fusion), channel_id=1, source_target_pairs={{0,64},{64,0},{1,65},{65,1},{2,66},{66,2},{3,67},{67,3},{4,68},{68... | collective-permute-start | bytes 5308424 | tf_op jit(solution)/shard_map/ppermute | solution.py:46
  254.3 61.8 %all-to-all-start.4 = ((bf16[4,64,768]{2,1,0:T(8,128)(2,1)}), bf16[4,64,768]{2,1,0:T(8,128)(2,1)}, u32[]{:S(2)}, u32[]{:S(2)}) async-start(bf16[4,64,768]{2,1,0:T(8,128)(2,1)} %broadcast_in_dim.121), calls=%async_computation.4 | async-start | bytes 786432 | tf_op jit(solution)/shard_map/all_to_all | solution.py:226
  281.5 14.1 %collective-permute-start.23 = (bf16[256,384]{1,0:T(8,128)(2,1)S(1)}, bf16[256,384]{1,0:T(8,128)(2,1)S(1)}, u32[]{:S(2)}, u32[]{:S(2)}) collective-permute-start(bf16[256,384]{1,0:T(8,128)(2,1)S(1)} %get-tuple-element.73), channel_id=1, source_target_pairs={{32,0},{36,4},{40,8},{44,12},{48,16},{52,20},{56,24},{60,28},{96,6... | collective-permute-start | bytes 589832 | tf_op jit(solution)/shard_map/ppermute | solution.py:42
  284.1 14.9 %collective-permute-start.25 = (bf16[256,384]{1,0:T(8,128)(2,1)S(1)}, bf16[256,384]{1,0:T(8,128)(2,1)S(1)}, u32[]{:S(2)}, u32[]{:S(2)}) collective-permute-start(bf16[256,384]{1,0:T(8,128)(2,1)S(1)} %get-tuple-element.75), channel_id=1, source_target_pairs={{16,0},{20,4},{24,8},{28,12},{32,16},{36,20},{40,24},{44,28},{48,3... | collective-permute-start | bytes 589832 | tf_op jit(solution)/shard_map/ppermute | solution.py:42
  285.4 13.6 %collective-permute-start.26 = (bf16[256,384]{1,0:T(8,128)(2,1)S(1)}, bf16[256,384]{1,0:T(8,128)(2,1)S(1)}, u32[]{:S(2)}, u32[]{:S(2)}) collective-permute-start(bf16[256,384]{1,0:T(8,128)(2,1)S(1)} %get-tuple-element.74), channel_id=1, source_target_pairs={{8,4},{12,0},{16,12},{20,8},{24,20},{28,16},{32,28},{36,24},{40,36... | collective-permute-start | bytes 589832 | tf_op jit(solution)/shard_map/ppermute | solution.py:42
  309.1 51.3 %collective-permute-start.28 = (bf16[16,24,2304]{2,1,0:T(8,128)(2,1)}, bf16[16,24,2304]{2,1,0:T(8,128)(2,1)}, u32[]{:S(2)}, u32[]{:S(2)}) collective-permute-start(bf16[16,24,2304]{2,1,0:T(8,128)(2,1)} %select_bitcast_fusion.1), channel_id=1, source_target_pairs={{0,64},{64,0},{1,65},{65,1},{2,66},{66,2},{3,67},{67,3},{4,68},{68... | collective-permute-start | bytes 5308424 | tf_op jit(solution)/shard_map/ppermute | solution.py:46
  327.6 41.2 %all-to-all-start.9 = ((bf16[16,32,2304]{2,1,0:T(8,128)(2,1)}), bf16[16,32,2304]{2,1,0:T(8,128)(2,1)}, u32[]{:S(2)}, u32[]{:S(2)}) async-start(bf16[16,32,2304]{2,1,0:T(8,128)(2,1)} %pad_maximum_fusion.3), calls=%async_computation.9 | async-start | bytes 4718592 | tf_op jit(solution)/shard_map/all_to_all | solution.py:434
  352.9 25.0 %collective-permute-start.14 = (bf16[2,256,768]{2,1,0:T(8,128)(2,1)}, bf16[2,256,768]{2,1,0:T(8,128)(2,1)}, u32[]{:S(2)}, u32[]{:S(2)}) collective-permute-start(bf16[2,256,768]{2,1,0:T(8,128)(2,1)} %pad_maximum_fusion.4), channel_id=1, source_target_pairs={{0,0},{4,64},{8,72},{12,8},{16,16},{20,80},{24,88},{28,24},{32,32}... | collective-permute-start | bytes 2359304 | tf_op jit(solution)/shard_map/ppermute | solution.py:42
  368.8 36.4 %all-to-all-start.8 = ((bf16[16,32,2304]{2,1,0:T(8,128)(2,1)}), bf16[16,32,2304]{2,1,0:T(8,128)(2,1)S(1)}, u32[]{:S(2)}, u32[]{:S(2)}) async-start(bf16[16,32,2304]{2,1,0:T(8,128)(2,1)} %pad_maximum_fusion.2), calls=%async_computation.8 | async-start | bytes 4718592 | tf_op jit(solution)/shard_map/all_to_all | solution.py:434
  385.6 47.2 %collective-permute-start.32 = (f32[256,768]{1,0:T(8,128)S(1)}, f32[256,768]{1,0:T(8,128)}, u32[]{:S(2)}, u32[]{:S(2)}) collective-permute-start(f32[256,768]{1,0:T(8,128)S(1)} %bitcast.165), channel_id=1, source_target_pairs={{0,0},{4,64},{8,72},{12,8},{16,16},{20,80},{24,88},{28,24},{32,32}... | collective-permute-start | bytes 2359304 | tf_op jit(solution)/shard_map/ppermute | solution.py:42
  390.9 23.7 %collective-permute-start.27 = (f32[64,768]{1,0:T(8,128)}, f32[64,768]{1,0:T(8,128)}, u32[]{:S(2)}, u32[]{:S(2)}) collective-permute-start(f32[64,768]{1,0:T(8,128)} %multiply_add_fusion), channel_id=1, source_target_pairs={{0,0},{4,64},{8,72},{12,8},{16,16},{20,80},{24,88},{28,24},{32,32}... | collective-permute-start | bytes 589832 | tf_op jit(solution)/shard_map/ppermute | solution.py:42
  416.6 16.2 %all-to-all-start.10 = ((f32[4,72,768]{2,1,0:T(8,128)}), f32[4,72,768]{2,1,0:T(8,128)S(1)}, u32[]{:S(2)}, u32[]{:S(2)}) async-start(f32[4,72,768]{2,1,0:T(8,128)} %broadcast_in_dim.131), calls=%async_computation.10 | async-start | bytes 1769472 | tf_op jit(solution)/shard_map/all_to_all | solution.py:226
  420.2 16.4 %collective-permute-start.34 = (f32[24,2304]{1,0:T(8,128)S(1)}, f32[24,2304]{1,0:T(8,128)}, u32[]{:S(2)}, u32[]{:S(2)}) collective-permute-start(f32[24,2304]{1,0:T(8,128)S(1)} %slice_select_fusion), channel_id=1, source_target_pairs={{0,64},{64,0},{1,65},{65,1},{2,66},{66,2},{3,67},{67,3},{4,68},{68... | collective-permute-start | bytes 663560 | tf_op jit(solution)/shard_map/ppermute | solution.py:46
  (103 other events, 1155.7 us)
Sparse Core Ops, SparseCore 0:
  10.7 66.6 all-gather.1
